TPU v7x, 256 devices: a whole 4x4x8 slice. The times are simulated.
256 devices in a mesh: replica: 8 (over y_lo, x), fsdp: 32 (over y_hi, z, core).
Axes of the slice: x: 4, y: 4 (y_hi: 2, y_lo: 2; y = y_hi * 2 + y_lo), z: 8, core: 2. Of those that a mesh axis runs over, the one named last changes fastest.
Arguments:
- hidden: bfloat16 [8, 4096, 8192], P('replica', 'fsdp'), may hold values from -6 to 6
- norm_gain: bfloat16 [8, 8192], P('replica', 'fsdp'), may hold values from 0.099609375 to 1.8984375
- key_value_weight: bfloat16 [8, 8192, 1024], P('replica', 'fsdp'), may hold values from -0.0625 to 0.0625
- upstream: bfloat16 [8, 4096, 1024], P('replica', 'fsdp'), may hold values from -6 to 6
- global_weight: float32 [8192, 1024], P('fsdp'), may hold values from -6 to 6
- global_momentum: float32 [8192, 1024], P('fsdp'), may hold values from -6 to 6
- replica_delta: float32 [8, 8192, 1024], P('replica', 'fsdp'), may hold values from -6 to 6
Outputs:
- keys_values: bfloat16 [8, 4096, 1024], P('replica', 'fsdp')
- input_gradient: bfloat16 [8, 4096, 8192], P('replica', 'fsdp')
- weight_gradient: bfloat16 [8, 8192, 1024], P('replica', 'fsdp')
- gain_gradient: bfloat16 [8, 8192], P('replica', 'fsdp')
- merged_weight: float32 [8192, 1024], P('fsdp')
- merged_momentum: float32 [8192, 1024], P('fsdp')
All inputs are finite; a program needn't handle non-finite values.
Results may differ from a plain program's by a relative error of at most 0.007.
Values may be sent and summed in bfloat16 or wider, within the bound.
A program may use at most 192 MiB of HBM per device.

v0:
```python
import jax
import jax.numpy as jnp
from jax import lax
from jax.sharding import PartitionSpec as P


def nesterov(weight, momentum, total, replicas):
    average = total / replicas
    fresh = 0.9 * momentum + average
    return (weight - 0.7 * (average + 0.9 * fresh), fresh)


def outer_step(global_weight, global_momentum, replica_delta):
    replicas = lax.axis_size("replica")
    total = lax.psum(replica_delta[0].astype(jnp.bfloat16), "replica").astype(jnp.float32)
    return nesterov(global_weight, global_momentum, total, replicas)


def local(
    hidden, norm_gain, key_value_weight, upstream, global_weight, global_momentum, replica_delta
):
    whole_weight, whole_gain = (
        lax.all_gather(key_value_weight[0], "fsdp", axis=0, tiled=True),
        lax.all_gather(norm_gain[0], "fsdp", axis=0, tiled=True),
    )
    tokens = hidden[0].astype(jnp.float32)
    square_mean = jnp.mean(tokens * tokens, axis=-1, keepdims=True)
    inverse = lax.rsqrt(square_mean + 1e-05)
    scaled = tokens * inverse
    gain_row = whole_gain.astype(jnp.float32)
    normed = (scaled * gain_row).astype(jnp.bfloat16)
    keys_values = jnp.dot(normed, whole_weight, preferred_element_type=jnp.float32).astype(
        jnp.bfloat16
    )
    cotangent = upstream[0]
    back = lax.dot_general(
        cotangent, whole_weight, (((1,), (1,)), ((), ())), preferred_element_type=jnp.float32
    )
    gain_partial = jnp.sum(back * scaled, axis=0)
    gain_share = lax.psum_scatter(gain_partial, "fsdp", scatter_dimension=0, tiled=True).astype(
        jnp.bfloat16
    )
    upper = back * gain_row
    inner = jnp.mean(upper * scaled, axis=-1, keepdims=True)
    input_gradient = (inverse * (upper - scaled * inner)).astype(jnp.bfloat16)
    columns = lax.all_to_all(normed, "fsdp", split_axis=1, concat_axis=0, tiled=True)
    every_cotangent = lax.all_gather(cotangent, "fsdp", axis=0, tiled=True)
    weight_gradient = lax.dot_general(
        columns, every_cotangent, (((0,), (0,)), ((), ())), preferred_element_type=jnp.float32
    )
    merged_weight, merged_momentum = outer_step(global_weight, global_momentum, replica_delta)
    return (
        keys_values[None],
        input_gradient[None],
        weight_gradient.astype(jnp.bfloat16)[None],
        gain_share[None],
        merged_weight,
        merged_momentum,
    )


def solution(mesh):
    placed = (
        P("replica", "fsdp", None),
        P("replica", "fsdp"),
        P("replica", "fsdp", None),
        P("replica", "fsdp", None),
        P("fsdp", None),
        P("fsdp", None),
        P("replica", "fsdp", None),
    )
    return jax.shard_map(
        local,
        mesh=mesh,
        in_specs=placed,
        out_specs=(
            P("replica", "fsdp", None),
            P("replica", "fsdp", None),
            P("replica", "fsdp", None),
            P("replica", "fsdp"),
            P("fsdp", None),
            P("fsdp", None),
        ),
        check_vma=False,
    )
```

profile of v0, /device:TPU:8, one launch (start us, length us, event | category | flops | bytes accessed | tf_op | source)
XLA Modules:
  0.0 446.7 jit_solution(5431410488475055856)
XLA Ops:
  8.0 0.0 copy-start
  8.0 0.0 all-reduce.3.cloned.1.call-start
  8.1 2.2 convert_bitcast_fusion
  10.3 0.0 copy-start.3
  10.3 0.0 all-reduce.3.cloned.1.call-update
  10.3 0.0 all-gather.8.cloned.1.call-start
  10.4 0.5 all-gather.8.cloned.1.call-update
  10.9 0.0 all-gather.6.cloned.1.call-start
  10.9 0.5 all-gather.6.cloned.1.call-update
  11.5 0.0 copy-done
  11.5 2.6 copy.15
  14.1 0.0 copy-done.3
  14.1 44.0 %all-gather = bf16[1,8192]{1,0:T(2,128)(2,1)S(1)} all-gather(bf16[1,256]{1,0:T(2,128)(2,1)S(1)} %copy-done.3), channel_id=2, replica_groups=mesh['replica'=8,'fsdp'=32] {'fsdp'}, dimensions={1}, use_global_device_ids=true | all-gather | bytes 16896 | tf_op jit(solution)/shard_map/all_gather | solution.py:24
  58.1 0.1 convert_reduce_fusion
  58.2 0.5 fusion.6
  58.7 0.0 copy-start.4
  58.7 0.0 copy-start.2
  58.7 6.1 %fusion.8 = bf16[128,32,256]{2,0,1:T(8,128)(2,1)} fusion(f32[128,32,256]{2,1,0:T(8,128)} %bitcast.62, f32[32,256]{1,0:T(8,128)S(1)} %mul.81, f32[128]{0:T(128)S(1)} %add_rsqrt_fusion), kind=kLoop, calls=%fused_computation.11 | loop fusion | flops 3145728 | bytes 6324736 | tf_op jit(solution)/shard_map/convert_element_type | solution.py:31
  64.8 4.8 %all-to-all-start = ((bf16[128,32,256]{2,0,1:T(8,128)(2,1)}), bf16[128,32,256]{2,0,1:T(8,128)(2,1)}, u32[]{:S(2)}, u32[]{:S(2)}) async-start(bf16[128,32,256]{2,0,1:T(8,128)(2,1)} %fusion.8), calls=%async_computation | async-start | bytes 4194304 | tf_op jit(solution)/shard_map/all_to_all | solution.py:46
  69.7 0.0 copy-done.4
  69.7 0.6 dynamic-slice
  71.0 23.6 %all-reduce.3.cloned.1.call-done = bf16[256,1024]{1,0:T(8,128)(2,1)} async-done(((bf16[256,1024]{1,0:T(8,128)(2,1)}), bf16[256,1024]{1,0:T(8,128)(2,1)}) %all-reduce.3.cloned.1.call-update) | async-done | bytes 524304 | tf_op jit(solution)/shard_map/psum | solution.py:15
  94.6 0.0 copy-done.2
  94.6 3.1 multiply_subtract_fusion
  97.6 26.3 %all-to-all-done = bf16[128,32,256]{2,0,1:T(8,128)(2,1)} async-done(((bf16[128,32,256]{2,0,1:T(8,128)(2,1)}), bf16[128,32,256]{2,0,1:T(8,128)(2,1)}, u32[]{:S(2)}, u32[]{:S(2)}) %all-to-all-start) | async-done | bytes 2097184 | tf_op jit(solution)/shard_map/all_to_all | solution.py:46
  123.9 20.8 %all-gather.8.cloned.1.call-done = bf16[1,4096,1024]{2,1,0:T(8,128)(2,1)} async-done(((bf16[1,128,1024]{2,1,0:T(8,128)(2,1)}), bf16[1,4096,1024]{2,1,0:T(8,128)(2,1)}) %all-gather.8.cloned.1.call-update) | async-done | bytes 8388624 | tf_op jit(solution)/shard_map/all_gather | solution.py:47
  144.7 0.0 copy-start.1
  144.7 7.2 %fusion.15 = bf16[1,256,1024]{2,1,0:T(8,128)(2,1)} fusion(bf16[4096,256]{1,0:T(8,128)(2,1)} %bitcast.7, bf16[1,4096,1024]{2,1,0:T(8,128)(2,1)} %all-gather.8.cloned.1.call-done), kind=kOutput, calls=%fused_computation.20 | convolution fusion | flops 2147745792 | bytes 11010048 | tf_op jit(solution)/shard_map/dot_general | solution.py:48
  151.9 129.1 %all-gather.6.cloned.1.call-done = bf16[1,8192,1024]{2,1,0:T(8,128)(2,1)} async-done(((bf16[1,256,1024]{2,1,0:T(8,128)(2,1)}), bf16[1,8192,1024]{2,1,0:T(8,128)(2,1)}) %all-gather.6.cloned.1.call-update) | async-done | bytes 16777232 | tf_op jit(solution)/shard_map/all_gather | solution.py:23
  281.0 0.0 copy-done.1
  281.0 13.7 %multiply_reduce_fusion = (f32[8192]{0:T(1024)S(1)}, f32[128]{0:T(128)S(1)}, f32[128,8192]{1,0:T(8,128)}) fusion(bf16[1,128,8192]{2,1,0:T(8,128)(2,1)S(1)} %copy-done, f32[128]{0:T(128)S(1)} %add_rsqrt_fusion, f32[8192]{0:T(1024)S(1)} %bitcast.63, bf16[1,8192,1024]{2,1,0:T(8,128)(2,1)} %all-gather.6.cloned.1.call-done, bf16[1,128,1024]{2,1,0:T(8,128)(2,1)S(1)} %copy-done.1), kind=kOutput, calls=%fused_computation.12 | convolution fusion | flops 2154815488 | bytes 23397376 | tf_op jit(solution)/shard_map/dot_general | solution.py:36
  294.6 130.7 %all-reduce = bf16[8192]{0:T(1024)(128)(2,1)S(1)} all-reduce(f32[8192]{0:T(1024)S(1)} %get-tuple-element.6), channel_id=5, replica_groups=mesh['replica'=8,'fsdp'=32] {'fsdp'}, use_global_device_ids=true, to_apply=%region_3.0.clone | all-reduce | flops 8192 | bytes 49152
  425.3 0.1 dynamic-slice.3
  425.4 0.6 broadcast_in_dim.19
  426.0 4.5 fusion.9
  430.4 8.9 %fusion.21 = bf16[1,128,1024]{2,1,0:T(8,128)(2,1)} fusion(bf16[1,8192,1024]{2,1,0:T(8,128)(2,1)} %all-gather.6.cloned.1.call-done, bf16[1,128,8192]{2,1,0:T(8,128)(2,1)S(1)} %copy-done, f32[8192]{0:T(1024)S(1)} %bitcast.65, f32[128]{0:T(128)S(1)} %add_rsqrt_fusion), kind=kOutput, calls=%fused_computation.22 | convolution fusion | flops 2151809024 | bytes 19169792 | tf_op jit(solution)/shard_map/dot_general | solution.py:32
  (4 shorter events, 0.1 us)
Async XLA Ops:
  8.0 3.5 copy-start
  8.0 86.5 %all-reduce.3.cloned.1.call-start = ((), (), s32[]{:S(2)}) async-start(), calls=%async_computation.1 | async-start | bytes 1048576 | tf_op jit(solution)/shard_map/psum | solution.py:15
  10.3 3.8 copy-start.3
  10.3 134.4 %all-gather.8.cloned.1.call-start = ((), (), s32[]{:S(2)}) async-start(), calls=%async_computation.3 | async-start | bytes 8650752 | tf_op jit(solution)/shard_map/all_gather | solution.py:47
  10.9 270.1 %all-gather.6.cloned.1.call-start = ((), (), s32[]{:S(2)}) async-start(), calls=%async_computation.2 | async-start | bytes 17301504 | tf_op jit(solution)/shard_map/all_gather | solution.py:23
  58.7 11.0 %copy-start.4 = (u32[256]{0:T(256)S(1)}, u32[256]{0:T(256)}, u32[]{:S(2)}) copy-start(u32[256]{0:T(256)} %constant.22) | copy-start | bytes 3076
  58.7 35.8 %copy-start.2 = (f32[256,1024]{1,0:T(8,128)S(1)}, f32[256,1024]{1,0:T(8,128)}, u32[]{:S(2)}) copy-start(f32[256,1024]{1,0:T(8,128)} %param.11) | copy-start | bytes 3145732
  64.8 59.1 %all-to-all-start = ((bf16[128,32,256]{2,0,1:T(8,128)(2,1)}), bf16[128,32,256]{2,0,1:T(8,128)(2,1)}, u32[]{:S(2)}, u32[]{:S(2)}) async-start(bf16[128,32,256]{2,0,1:T(8,128)(2,1)} %fusion.8), calls=%async_computation | async-start | bytes 4194304 | tf_op jit(solution)/shard_map/all_to_all | solution.py:46
  144.7 136.3 %copy-start.1 = (bf16[1,128,1024]{2,1,0:T(8,128)(2,1)S(1)}, bf16[1,128,1024]{2,1,0:T(8,128)(2,1)}, u32[]{:S(2)}) copy-start(bf16[1,128,1024]{2,1,0:T(8,128)(2,1)} %param.10) | copy-start | bytes 786436
Sparse Core Ops, SparseCore 0:
  12.0 82.4 all-reduce.2
Sparse Core Ops, SparseCore 1:
  13.6 131.1 all-gather.7
  147.3 133.6 all-gather.5
where the time goes:
time: 447 us
  waiting for transfers between devices  201 us (45%)
  blocking collectives  175 us (39%)
  matrix products  29.7 us (7%)
  other arithmetic  16.5 us (4%)
  between operations  16.2 us (4%)
  starting transfers between devices  4.93 us (1%)
    unnamed x1, blocking collectives  131 us
    all_gather x1, waiting for transfers between devices, local(): lax.all_gather(key_value_weight[0], 'fsdp', axis=0, tiled=True)  129 us
    all_gather x1, blocking collectives, local(): lax.all_gather(norm_gain[0], 'fsdp', axis=0, tiled=True)  44 us
    all_to_all x1, waiting for transfers between devices, local(): lax.all_to_all(normed, 'fsdp', split_axis=1, concat_axis=0, tiled=True)  26.3 us
    psum x1, waiting for transfers between devices, outer_step(): lax.psum(replica_delta[0].astype(jnp.bfloat16), 'replica')  23.6 us
    all_gather x1, waiting for transfers between devices, local(): every_cotangent = lax.all_gather(cotangent, 'fsdp', axis=0, tiled=True)  20.8 us
    dot_general x1, matrix products, local(): lax.dot_general(cotangent, whole_weight, (((1,), (1,)), ((), ())), prefer...  13.7 us
  transfers between devices with their start and end apart: 4, of which 4 were waited for; matrix products, arithmetic and copies ran while one was open for 5% of the time, Pallas kernels for 0%

commit v1 on v0

v1 whole, which is shorter than its diff:
```python
import functools

import jax
import jax.numpy as jnp
from jax import lax
from jax.experimental import pallas as pl
from jax.experimental.pallas import tpu as pltpu
from jax.sharding import PartitionSpec as P

MESH = pl.DeviceIdType.MESH
F32 = jnp.float32
BF16 = jnp.bfloat16
T = 128
F = 256
K = 1024
D = 8192
R = 64


def device(h, z, c, low, x):
    return {"replica": low * 4 + x, "fsdp": h * 16 + z * 2 + c}


def kernel(
    x_hbm, gain_ref, w_hbm, u_hbm, delta_hbm, gw_hbm, gm_hbm,
    kv_out, dx_out, dw_out, gg_out, mw_out, mm_out,
    xv, xq, wv, wq, uv, uall, ub, uh, inv, gcol, rs_out, rs_in,
    kvs, kvr, gps, gpr, dv, dbf, d1, d2s, d2r, davg, gwv, gmv, dxv, dwv, kvv,
    ld, lq, st, ag_s, ag_r, rs_s, rs_r, x_s, x_r, u_s, u_r, b_s, b_r, k_s, k_r, g_s, g_r,
    d1_s, d1_r, d2_s, d2_r, d3_s, d3_r,
):
    fsdp, rep = lax.axis_index("fsdp"), lax.axis_index("replica")
    h, z, c = fsdp // 16, (fsdp % 16) // 2, fsdp % 2
    low, xx = rep // 4, rep % 4

    def mate(k):
        return device((h + k // 2) % 2, z, (c + k % 2) % 2, low, xx)

    def along(step):
        return device(h, (z + 8 + step) % 8, c, low, xx)

    def column(k, j):
        at = ((h + k // 2) % 2) * 4096 + j * 512 + ((c + k % 2) % 2) * 256
        return pl.ds(pl.multiple_of(at, 256), 256)

    def remote(src, dst, s, r, to):
        return pltpu.make_async_remote_copy(
            src_ref=src, dst_ref=dst, send_sem=s, recv_sem=r, device_id=to, device_id_type=MESH
        )

    load_w = pltpu.make_async_copy(w_hbm, wv, ld.at[0])
    load_u = pltpu.make_async_copy(u_hbm, uv, ld.at[1])
    load_x = pltpu.make_async_copy(x_hbm, xv, ld.at[2])
    load_d = pltpu.make_async_copy(delta_hbm, dv, ld.at[3])
    load_gw = pltpu.make_async_copy(gw_hbm, gwv, ld.at[4])
    load_gm = pltpu.make_async_copy(gm_hbm, gmv, ld.at[5])
    load_w.start()
    load_x.start()
    load_u.start()
    load_d.start()

    def own_x(j):
        return pltpu.make_async_copy(x_hbm.at[:, column(0, j)], xq.at[j, pl.ds(0, T)], lq.at[j])

    barrier = pltpu.get_barrier_semaphore()
    others = [along(s) for s in range(1, 8)] + [mate(k) for k in range(1, 4)]
    others += [device(h, z, c, low, (xx + q) % 4) for q in range(1, 4)]
    others += [device(h, z, c, 1 - low, xx)]
    for to in others:
        pl.semaphore_signal(barrier, inc=1, device_id=to, device_id_type=MESH)

    gain_row = gain_ref[...].astype(F32)
    gcol[...] = jnp.transpose(jnp.broadcast_to(gain_row, (128, F)))
    load_w.wait()
    for half in range(2):
        rows = pl.ds(half * 128, 128)
        g = gcol[rows, :]
        for t in range(8):
            cols = pl.ds(t * 128, 128)
            wq[z, half, :, cols] = (wv[rows, cols].astype(F32) * g).astype(BF16)
    pl.semaphore_wait(barrier, len(others))

    chains = [(1, 0, 0), (-1, 1, 0), (1, 1, 1), (-1, 0, 1)]

    def gather(n, chain):
        sign, half, short = chain
        d = 0 if sign > 0 else 1
        block = wq.at[(z + 8 - sign * (n - 1)) % 8, half]
        return remote(block, block, ag_s.at[d, n - 1, half], ag_r.at[d, n - 1, half], along(sign))

    def gather_in(n, chain):
        sign, half, short = chain
        d = 0 if sign > 0 else 1
        block = wq.at[(z + 8 - sign * n) % 8, half]
        return remote(block, block, ag_s.at[d, n - 1, half], ag_r.at[d, n - 1, half], along(sign))

    for chain in chains:
        gather(1, chain).start()

    def x_copy(k, j):
        return remote(
            x_hbm.at[:, column(k, j)], xq.at[j, pl.ds(k * T, T)], x_s.at[k - 1, j], x_r.at[k - 1, j], mate(k)
        )

    @pl.loop(0, 8)
    def _(j):
        for k in (2, 3, 1):
            x_copy(k, j).start()
        own_x(j).start()

    def quarter(i):
        return pl.ds(pl.multiple_of(i * R, R), R)

    def d1_copy(q):
        to = (xx + q) % 4
        return remote(dbf.at[quarter(to)], d1.at[q - 1], d1_s.at[q - 1], d1_r.at[q - 1], device(h, z, c, low, to))

    load_d.wait()
    dbf[...] = dv[...].astype(BF16)
    for q in range(1, 4):
        d1_copy(q).start()

    load_x.wait()

    def squares(i, acc):
        v = xv[:, pl.ds(pl.multiple_of(i * 256, 256), 256)].astype(F32)
        return acc + v * v

    acc = lax.fori_loop(0, 32, squares, jnp.zeros((T, 256), F32))
    inverse = lax.rsqrt(jnp.sum(acc, axis=1, keepdims=True) * (1.0 / D) + 1e-05)
    inv[...] = jnp.broadcast_to(inverse, (T, 128))
    load_u.wait()
    uall[pl.ds(0, T), :] = (uv[...].astype(F32) * inverse).astype(BF16)

    def u_copy(k):
        return remote(uall.at[pl.ds(0, T)], uall.at[pl.ds(k * T, T)], u_s.at[k - 1], u_r.at[k - 1], mate(k))

    for k in (2, 3, 1):
        u_copy(k).start()
    load_gw.start()
    load_gm.start()

    def hop(n):
        for chain in chains:
            gather_in(n, chain).wait_recv()
            if n < 3 or chain[2] == 0:
                gather(n + 1, chain).start()

    hop(1)

    d2_copy = remote(d2s, d2r, d2_s, d2_r, device(h, z, c, 1 - low, xx))
    for q in range(1, 4):
        d1_copy(q).wait_recv()
    d2s[...] = (
        dv[quarter(xx), :] + d1[0].astype(F32) + d1[1].astype(F32) + d1[2].astype(F32)
    ).astype(BF16)
    d2_copy.start()

    hop(2)

    def d3_copy(q):
        block = davg.at[quarter(xx)]
        return remote(block, block, d3_s.at[q - 1], d3_r.at[q - 1], device(h, z, c, low, (xx + q) % 4))

    d2_copy.wait_recv()
    davg[quarter(xx), :] = ((d2s[...].astype(F32) + d2r[...].astype(F32)) * 0.125).astype(BF16)
    for q in range(1, 4):
        d3_copy(q).start()

    hop(3)

    def d3_in(q):
        block = davg.at[quarter((xx + 4 - q) % 4)]
        return remote(block, block, d3_s.at[q - 1], d3_r.at[q - 1], device(h, z, c, low, (xx + q) % 4))

    for q in range(1, 4):
        d3_in(q).wait_recv()
    load_gw.wait()
    load_gm.wait()

    @pl.loop(0, 8)
    def _(i):
        rows = pl.ds(pl.multiple_of(i * 32, 32), 32)
        average = davg[rows, :].astype(F32)
        fresh = 0.9 * gmv[rows, :] + average
        gmv[rows, :] = fresh
        gwv[rows, :] = gwv[rows, :] - 0.7 * (average + 0.9 * fresh)

    store_mw = pltpu.make_async_copy(gwv, mw_out, st.at[0])
    store_mm = pltpu.make_async_copy(gmv, mm_out, st.at[1])
    store_mw.start()
    store_mm.start()

    def partial(j, half):
        return lax.dot_general(
            xq[j, :, pl.ds(half * 128, 128)], uall[...], (((0,), (0,)), ((), ())), preferred_element_type=F32
        )

    def reduce(n, chain):
        sign, half, short = chain
        d = 0 if sign > 0 else 1
        return remote(
            rs_out.at[d, n - 1, short], rs_in.at[d, n - 1, short],
            rs_s.at[d, n - 1, short], rs_r.at[d, n - 1, short], along(sign),
        )

    def send_sum(n, chain):
        sign, half, short = chain
        d = 0 if sign > 0 else 1
        j = (z + 8 + sign * (5 - short - n)) % 8
        value = partial(j, half)
        if n > 1:
            reduce(n - 1, chain).wait_recv()
            value = value + rs_in[d, n - 2, short].astype(F32)
        rs_out[d, n - 1, short] = value.astype(BF16)
        reduce(n, chain).start()

    for k in (1, 2, 3):
        u_copy(k).wait_recv()

    @pl.loop(0, 8)
    def _(j):
        own_x(j).wait()
        for k in (1, 2, 3):
            x_copy(k, j).wait_recv()

    for chain in chains:
        send_sum(1, chain)

    for chain in chains[:2]:
        gather_in(4, chain).wait_recv()

    def b_copy(k, j):
        return remote(ub.at[j, k], uh.at[k, j], b_s.at[k - 1, j], b_r.at[k - 1, j], mate(k))

    @pl.loop(0, 8)
    def _(j):
        w = wq[j].reshape(F, K)
        u = lax.dot_general(uall[...], w, (((1,), (1,)), ((), ())), preferred_element_type=F32)
        ub[j] = u.astype(BF16).reshape(4, T, F)
        for k in (2, 3, 1):
            b_copy(k, j).start()
        gps[j] = jnp.sum(u * xq[j].astype(F32), axis=0, keepdims=True)

    def g_copy(s):
        return remote(gps.at[(z + s) % 8], gpr.at[s - 1], g_s.at[s - 1], g_r.at[s - 1], along(s))

    for s in range(1, 8):
        g_copy(s).start()

    for chain in chains:
        send_sum(2, chain)

    def k_copy(k):
        return remote(kvs.at[k], kvr.at[k - 1], k_s.at[k - 1], k_r.at[k - 1], mate(k))

    def kv_part(k):
        def add(j, acc):
            return acc + jnp.dot(
                xq[j, pl.ds(k * T, T), :], wq[j].reshape(F, K), preferred_element_type=F32
            )

        return lax.fori_loop(0, 8, add, jnp.zeros((T, K), F32))

    for k in (2, 3, 1):
        kvs[k] = kv_part(k).astype(BF16)
        k_copy(k).start()
    kvv[...] = kv_part(0)

    for chain in chains:
        send_sum(3, chain)

    @pl.loop(0, 8)
    def _(j):
        for k in (1, 2, 3):
            b_copy(k, j).wait_recv()

    def dots(j, acc):
        acc = acc + xv[:, column(0, j)].astype(F32) * ub[j, 0].astype(F32)
        for k in (1, 2, 3):
            acc = acc + xv[:, column(k, j)].astype(F32) * uh[k, j].astype(F32)
        return acc

    acc = lax.fori_loop(0, 8, dots, jnp.zeros((T, 256), F32))
    inverse = inv[...][:, :1]
    coefficient = jnp.sum(acc, axis=1, keepdims=True) * (1.0 / D) * inverse * inverse

    @pl.loop(0, 8)
    def _(j):
        for k in range(4):
            u = (ub[j, 0] if k == 0 else uh[k, j]).astype(F32)
            dxv[:, column(k, j)] = (u - xv[:, column(k, j)].astype(F32) * coefficient).astype(BF16)

    store_dx = pltpu.make_async_copy(dxv, dx_out, st.at[2])
    store_dx.start()

    for chain in chains[:2]:
        send_sum(4, chain)

    for k in (1, 2, 3):
        k_copy(k).wait_recv()
    total = kvv[...] + kvr[0].astype(F32) + kvr[1].astype(F32) + kvr[2].astype(F32)
    uv[...] = (total * inverse).astype(BF16)
    store_kv = pltpu.make_async_copy(uv, kv_out, st.at[3])
    store_kv.start()

    gain_sum = gps[z]
    for s in range(1, 8):
        g_copy(s).wait_recv()
    for s in range(1, 8):
        gain_sum = gain_sum + gpr[s - 1]
    gg_out[...] = gain_sum / gain_row

    for half in range(2):
        rows = pl.ds(half * 128, 128)
        value = partial(z, half)
        for chain in chains:
            if chain[1] == half:
                sign, _, short = chain
                d = 0 if sign > 0 else 1
                reduce(4 - short, chain).wait_recv()
                value = value + rs_in[d, 3 - short, short].astype(F32)
        g = gcol[rows, :]
        for t in range(8):
            dwv[rows, pl.ds(t * 128, 128)] = (value[:, t * 128 : t * 128 + 128] * g).astype(BF16)
    store_dw = pltpu.make_async_copy(dwv, dw_out, st.at[4])
    store_dw.start()

    for chain in chains:
        for n in range(1, 5 - chain[2]):
            gather(n, chain).wait_send()
            reduce(n, chain).wait_send()
    for k in (1, 2, 3):
        u_copy(k).wait_send()
        k_copy(k).wait_send()

    @pl.loop(0, 8)
    def _(j):
        for k in (1, 2, 3):
            x_copy(k, j).wait_send()
            b_copy(k, j).wait_send()

    for s in range(1, 8):
        g_copy(s).wait_send()
    for q in range(1, 4):
        d1_copy(q).wait_send()
        d3_copy(q).wait_send()
    d2_copy.wait_send()
    store_mw.wait()
    store_mm.wait()
    store_dx.wait()
    store_kv.wait()
    store_dw.wait()


def local(hidden, norm_gain, weight, upstream, global_weight, global_momentum, replica_delta):
    anywhere = pl.BlockSpec(memory_space=pl.ANY)
    in_vmem = pl.BlockSpec(memory_space=pltpu.VMEM)
    dma = pltpu.SemaphoreType.DMA
    kv, dx, dw, gg, mw, mm = pl.pallas_call(
        kernel,
        out_shape=(
            jax.ShapeDtypeStruct((T, K), BF16),
            jax.ShapeDtypeStruct((T, D), BF16),
            jax.ShapeDtypeStruct((F, K), BF16),
            jax.ShapeDtypeStruct((1, F), F32),
            jax.ShapeDtypeStruct((F, K), F32),
            jax.ShapeDtypeStruct((F, K), F32),
        ),
        in_specs=[anywhere, in_vmem] + [anywhere] * 5,
        out_specs=(anywhere, anywhere, anywhere, in_vmem, anywhere, anywhere),
        scratch_shapes=[
            pltpu.VMEM((T, D), BF16),
            pltpu.VMEM((8, 4 * T, F), BF16),
            pltpu.VMEM((F, K), BF16),
            pltpu.VMEM((8, 2, 128, K), BF16),
            pltpu.VMEM((T, K), BF16),
            pltpu.VMEM((4 * T, K), BF16),
            pltpu.VMEM((8, 4, T, F), BF16),
            pltpu.VMEM((4, 8, T, F), BF16),
            pltpu.VMEM((T, 128), F32),
            pltpu.VMEM((F, 128), F32),
            pltpu.VMEM((2, 4, 2, 128, K), BF16),
            pltpu.VMEM((2, 4, 2, 128, K), BF16),
            pltpu.VMEM((4, T, K), BF16),
            pltpu.VMEM((3, T, K), BF16),
            pltpu.VMEM((8, 1, F), F32),
            pltpu.VMEM((7, 1, F), F32),
            pltpu.VMEM((F, K), F32),
            pltpu.VMEM((F, K), BF16),
            pltpu.VMEM((3, R, K), BF16),
            pltpu.VMEM((R, K), BF16),
            pltpu.VMEM((R, K), BF16),
            pltpu.VMEM((F, K), BF16),
            pltpu.VMEM((F, K), F32),
            pltpu.VMEM((F, K), F32),
            pltpu.VMEM((T, D), BF16),
            pltpu.VMEM((F, K), BF16),
            pltpu.VMEM((T, K), F32),
            dma((6,)), dma((8,)), dma((5,)),
            dma((2, 4, 2)), dma((2, 4, 2)), dma((2, 4, 2)), dma((2, 4, 2)),
            dma((3, 8)), dma((3, 8)), dma((3,)), dma((3,)), dma((3, 8)), dma((3, 8)),
            dma((3,)), dma((3,)), dma((7,)), dma((7,)),
            dma((3,)), dma((3,)), dma, dma, dma((3,)), dma((3,)),
        ],
        compiler_params=pltpu.CompilerParams(
            collective_id=0, has_side_effects=True, vmem_limit_bytes=58 * 2**20
        ),
        cost_estimate=pl.CostEstimate(flops=6442450944, bytes_accessed=14 * 2**20, transcendentals=0),
        name="project",
    )(
        hidden[0], norm_gain, weight[0], upstream[0], replica_delta[0], global_weight, global_momentum
    )
    return kv[None], dx[None], dw[None], gg.astype(BF16), mw, mm


def solution(mesh):
    rows = P("replica", "fsdp", None)
    return jax.shard_map(
        local,
        mesh=mesh,
        in_specs=(rows, P("replica", "fsdp"), rows, rows, P("fsdp", None), P("fsdp", None), rows),
        out_specs=(rows, rows, rows, P("replica", "fsdp"), P("fsdp", None), P("fsdp", None)),
        check_vma=False,
    )
```

time: 447 us -> 111 us (0.25)
  waiting for transfers between devices: 201 us -> 0 us
  blocking collectives: 175 us -> 0 us
  Pallas kernels: 0 us -> 102 us
  matrix products: 29.7 us -> 0 us
  between operations: 16.2 us -> 0.65 us
  other arithmetic: 16.5 us -> 1.24 us
  starting transfers between devices: 4.93 us -> 0 us
    all_gather x2 -> x0, waiting for transfers between devices: 150 us -> none  [the longest x1 129 us: local(): lax.all_gather(key_value_weight[0], 'fsdp', axis=0, tiled=True)]
    unnamed x1 -> x0, blocking collectives: 131 us -> none
    pallas_call x0 -> x1, Pallas kernels: none -> 102 us  [local(): pl.pallas_call(kernel, out_shape=(jax.ShapeDtypeStruct((T, K), BF16), jax...]
    all_gather x1 -> x0, blocking collectives: 44 us -> none  [local(): lax.all_gather(norm_gain[0], 'fsdp', axis=0, tiled=True)]
    dot_general x3 -> x0, matrix products: 29.7 us -> none  [the longest x1 13.7 us: local(): lax.dot_general(cotangent, whole_weight, (((1,), (1,)), ((), ())), prefer...]
    all_to_all x1 -> x0, waiting for transfers between devices: 26.3 us -> none  [local(): lax.all_to_all(normed, 'fsdp', split_axis=1, concat_axis=0, tiled=True)]
    psum x1 -> x0, waiting for transfers between devices: 23.6 us -> none  [outer_step(): lax.psum(replica_delta[0].astype(jnp.bfloat16), 'replica')]
    convert_element_type x4 -> x1, other arithmetic: 8.47 us -> 1.24 us  [local(): return (kv[None], dx[None], dw[None], gg.astype(BF16), mw, mm)]
  transfers between devices with their start and end apart: 4 -> 0, of which waited for: 4 -> 0; matrix products, arithmetic and copies ran while one was open for 5% -> 0% of each run, Pallas kernels for 0% -> 0%
where the time goes in v1:
time: 111 us
  Pallas kernels  102 us (92%)
  local copies, waits for them, and re-layouts  7.63 us (7%)
  other arithmetic  1.24 us (1%)
    pallas_call x1, Pallas kernels, local(): pl.pallas_call(kernel, out_shape=(jax.ShapeDtypeStruct((T, K), BF16), jax...  102 us
    unnamed x11, local copies, waits for them, and re-layouts  7.63 us

profile of v1, /device:TPU:8, one launch (start us, length us, event | category | flops | bytes accessed | tf_op | source)
XLA Modules:
  0.0 111.1 jit_solution(5174195160468136167)
XLA Ops:
  0.6 101.6 %project.1 = (bf16[128,1024]{1,0:T(8,128)(2,1)}, bf16[128,8192]{1,0:T(8,128)(2,1)}, bf16[256,1024]{1,0:T(8,128)(2,1)}, f32[1,256]{1,0:T(1,128)}, f32[256,1024]{1,0:T(8,128)}, /*index=5*/f32[256,1024]{1,0:T(8,128)}) custom-call(bf16[128,8192]{1,0:T(8,128)(2,1)} %bitcast.10, bf16[1,256]{1,0:T(2,128)(2,1)} %gain_ref.1, bf16[256,1024]{1,0:T(8,128)(2,1)} %bitcast.12, ...), custom_call_target="tpu_custom_call" | custom-call | flops 6442450944 | bytes 14680064 | tf_op jit(solution)/shard_map/project/pallas_call | solution.py:360
  102.2 1.2 %convert_element_type.3 = bf16[1,256]{1,0:T(2,128)(2,1)} convert(f32[1,256]{1,0:T(1,128)} %get-tuple-element.15) | non-fusion elementwise | flops 256 | bytes 1536 | tf_op jit(solution)/shard_map/convert_element_type | solution.py:414
  103.5 1.7 %copy.18 = bf16[1,128,1024]{2,1,0:T(8,128)(2,1)} copy(bf16[1,128,1024]{2,1,0:T(8,128)(2,1)} %bitcast.9) | data formatting | bytes 524288
  105.2 0.0 copy-start.2
  105.2 0.0 copy-start.1
  105.2 3.2 %copy.19 = bf16[1,128,8192]{2,1,0:T(8,128)(2,1)} copy(bf16[1,128,8192]{2,1,0:T(8,128)(2,1)} %bitcast.7) | data formatting | bytes 4194304
  108.4 0.0 copy-done.2
  108.4 0.0 copy-start
  108.4 0.8 copy.20
  109.2 0.0 copy-done.1
  109.2 1.0 copy.21
  110.2 0.0 copy-done
  110.2 1.0 copy.22
Async XLA Ops:
  105.2 3.2 %copy-start.2 = (bf16[256,1024]{1,0:T(8,128)(2,1)S(1)}, bf16[256,1024]{1,0:T(8,128)(2,1)}, u32[]{:S(2)}) copy-start(bf16[256,1024]{1,0:T(8,128)(2,1)} %get-tuple-element.14) | copy-start | bytes 1572868
  105.2 4.0 %copy-start.1 = (f32[256,1024]{1,0:T(8,128)S(1)}, f32[256,1024]{1,0:T(8,128)}, u32[]{:S(2)}) copy-start(f32[256,1024]{1,0:T(8,128)} %get-tuple-element.28) | copy-start | bytes 3145732
  108.4 1.8 %copy-start = (f32[256,1024]{1,0:T(8,128)S(1)}, f32[256,1024]{1,0:T(8,128)}, u32[]{:S(2)}) copy-start(f32[256,1024]{1,0:T(8,128)} %get-tuple-element.29) | copy-start | bytes 3145732

commit v2 on v1

--- a/solution.py
+++ b/solution.py
@@ -25,8 +25,8 @@
     x_hbm, gain_ref, w_hbm, u_hbm, delta_hbm, gw_hbm, gm_hbm,
     kv_out, dx_out, dw_out, gg_out, mw_out, mm_out,
     xv, xq, wv, wq, uv, uall, ub, uh, inv, gcol, rs_out, rs_in,
-    kvs, kvr, gps, gpr, dv, dbf, d1, d2s, d2r, davg, gwv, gmv, dxv, dwv, kvv,
-    ld, lq, st, ag_s, ag_r, rs_s, rs_r, x_s, x_r, u_s, u_r, b_s, b_r, k_s, k_r, g_s, g_r,
+    kvs, kvr, gps, gpr, dv, dbf, d1, d2s, d2r, davg, gwv, gmv, kvv,
+    ld, lq, ag_s, ag_r, rs_s, rs_r, x_s, x_r, u_s, u_r, b_s, b_r, k_s, k_r, g_s, g_r,
     d1_s, d1_r, d2_s, d2_r, d3_s, d3_r,
 ):
     fsdp, rep = lax.axis_index("fsdp"), lax.axis_index("replica")
@@ -102,11 +102,10 @@
             x_hbm.at[:, column(k, j)], xq.at[j, pl.ds(k * T, T)], x_s.at[k - 1, j], x_r.at[k - 1, j], mate(k)
         )
 
-    @pl.loop(0, 8)
-    def _(j):
-        for k in (2, 3, 1):
+    @pl.loop(0, 2)
+    def _(j):
+        for k in (2, 3):
             x_copy(k, j).start()
-        own_x(j).start()
 
     def quarter(i):
         return pl.ds(pl.multiple_of(i * R, R), R)
@@ -133,12 +132,48 @@
     uall[pl.ds(0, T), :] = (uv[...].astype(F32) * inverse).astype(BF16)
 
     def u_copy(k):
-        return remote(uall.at[pl.ds(0, T)], uall.at[pl.ds(k * T, T)], u_s.at[k - 1], u_r.at[k - 1], mate(k))
-
-    for k in (2, 3, 1):
-        u_copy(k).start()
+        near = 2 * T if k == 3 else 0
+        to = mate(1) if k == 3 else mate(k)
+        return remote(uall.at[pl.ds(near, T)], uall.at[pl.ds(k * T, T)], u_s.at[k - 1], u_r.at[k - 1], to)
+
+    u_copy(2).start()
+    u_copy(1).start()
+
+    @pl.loop(2, 8)
+    def _(j):
+        for k in (2, 3):
+            x_copy(k, j).start()
+
+    @pl.loop(0, 8)
+    def _(j):
+        x_copy(1, j).start()
+        own_x(j).start()
+
     load_gw.start()
     load_gm.start()
+
+    def b_copy(k, j):
+        return remote(ub.at[j, k], uh.at[k, j], b_s.at[k - 1, j], b_r.at[k - 1, j], mate(k))
+
+    def upper(low_step, high_step):
+        @pl.loop(low_step, high_step)
+        def _(step):
+            j = (z + 8 + step) % 8
+            w = wq[j].reshape(F, K)
+            u = lax.dot_general(uall[...], w, (((1,), (1,)), ((), ())), preferred_element_type=F32)
+            ub[j] = u.astype(BF16).reshape(4, T, F)
+            for k in (2, 3, 1):
+                b_copy(k, j).start()
+
+    def upper_pair(step):
+        @pl.loop(0, 2)
+        def _(i):
+            j = (z + 8 + step - 2 * step * i) % 8
+            w = wq[j].reshape(F, K)
+            u = lax.dot_general(uall[...], w, (((1,), (1,)), ((), ())), preferred_element_type=F32)
+            ub[j] = u.astype(BF16).reshape(4, T, F)
+            for k in (2, 3, 1):
+                b_copy(k, j).start()
 
     def hop(n):
         for chain in chains:
@@ -156,6 +191,12 @@
     ).astype(BF16)
     d2_copy.start()
 
+    u_copy(2).wait_recv()
+    u_copy(3).start()
+    u_copy(1).wait_recv()
+    u_copy(3).wait_recv()
+    upper(-1, 2)
+
     hop(2)
 
     def d3_copy(q):
@@ -166,8 +207,10 @@
     davg[quarter(xx), :] = ((d2s[...].astype(F32) + d2r[...].astype(F32)) * 0.125).astype(BF16)
     for q in range(1, 4):
         d3_copy(q).start()
+    upper_pair(2)
 
     hop(3)
+    upper_pair(3)
 
     def d3_in(q):
         block = davg.at[quarter((xx + 4 - q) % 4)]
@@ -183,13 +226,8 @@
         rows = pl.ds(pl.multiple_of(i * 32, 32), 32)
         average = davg[rows, :].astype(F32)
         fresh = 0.9 * gmv[rows, :] + average
-        gmv[rows, :] = fresh
-        gwv[rows, :] = gwv[rows, :] - 0.7 * (average + 0.9 * fresh)
-
-    store_mw = pltpu.make_async_copy(gwv, mw_out, st.at[0])
-    store_mm = pltpu.make_async_copy(gmv, mm_out, st.at[1])
-    store_mw.start()
-    store_mm.start()
+        mm_out[rows, :] = fresh
+        mw_out[rows, :] = gwv[rows, :] - 0.7 * (average + 0.9 * fresh)
 
     def partial(j, half):
         return lax.dot_general(
@@ -215,9 +253,6 @@
         rs_out[d, n - 1, short] = value.astype(BF16)
         reduce(n, chain).start()
 
-    for k in (1, 2, 3):
-        u_copy(k).wait_recv()
-
     @pl.loop(0, 8)
     def _(j):
         own_x(j).wait()
@@ -230,16 +265,11 @@
     for chain in chains[:2]:
         gather_in(4, chain).wait_recv()
 
-    def b_copy(k, j):
-        return remote(ub.at[j, k], uh.at[k, j], b_s.at[k - 1, j], b_r.at[k - 1, j], mate(k))
-
-    @pl.loop(0, 8)
-    def _(j):
-        w = wq[j].reshape(F, K)
-        u = lax.dot_general(uall[...], w, (((1,), (1,)), ((), ())), preferred_element_type=F32)
-        ub[j] = u.astype(BF16).reshape(4, T, F)
-        for k in (2, 3, 1):
-            b_copy(k, j).start()
+    upper(4, 5)
+
+    @pl.loop(0, 8)
+    def _(j):
+        u = ub[j].reshape(4 * T, F).astype(F32)
         gps[j] = jnp.sum(u * xq[j].astype(F32), axis=0, keepdims=True)
 
     def g_copy(s):
@@ -252,7 +282,8 @@
         send_sum(2, chain)
 
     def k_copy(k):
-        return remote(kvs.at[k], kvr.at[k - 1], k_s.at[k - 1], k_r.at[k - 1], mate(k))
+        to = mate(1) if k == 3 else mate(k)
+        return remote(kvs.at[k], kvr.at[k - 1], k_s.at[k - 1], k_r.at[k - 1], to)
 
     def kv_part(k):
         def add(j, acc):
@@ -262,9 +293,14 @@
 
         return lax.fori_loop(0, 8, add, jnp.zeros((T, K), F32))
 
-    for k in (2, 3, 1):
-        kvs[k] = kv_part(k).astype(BF16)
-        k_copy(k).start()
+    kvs[3] = kv_part(3).astype(BF16)
+    k_copy(3).start()
+    kvs[1] = kv_part(1).astype(BF16)
+    k_copy(1).start()
+    value = kv_part(2)
+    k_copy(3).wait_recv()
+    kvs[2] = (value + kvr[2].astype(F32)).astype(BF16)
+    k_copy(2).start()
     kvv[...] = kv_part(0)
 
     for chain in chains:
@@ -289,27 +325,22 @@
     def _(j):
         for k in range(4):
             u = (ub[j, 0] if k == 0 else uh[k, j]).astype(F32)
-            dxv[:, column(k, j)] = (u - xv[:, column(k, j)].astype(F32) * coefficient).astype(BF16)
-
-    store_dx = pltpu.make_async_copy(dxv, dx_out, st.at[2])
-    store_dx.start()
+            dx_out[:, column(k, j)] = (u - xv[:, column(k, j)].astype(F32) * coefficient).astype(BF16)
 
     for chain in chains[:2]:
         send_sum(4, chain)
 
-    for k in (1, 2, 3):
+    for k in (1, 2):
         k_copy(k).wait_recv()
-    total = kvv[...] + kvr[0].astype(F32) + kvr[1].astype(F32) + kvr[2].astype(F32)
-    uv[...] = (total * inverse).astype(BF16)
-    store_kv = pltpu.make_async_copy(uv, kv_out, st.at[3])
-    store_kv.start()
+    total = kvv[...] + kvr[0].astype(F32) + kvr[1].astype(F32)
+    kv_out[...] = (total * inverse).astype(BF16)
 
     gain_sum = gps[z]
     for s in range(1, 8):
         g_copy(s).wait_recv()
     for s in range(1, 8):
         gain_sum = gain_sum + gpr[s - 1]
-    gg_out[...] = gain_sum / gain_row
+    gg_out[...] = (gain_sum / gain_row).astype(BF16)
 
     for half in range(2):
         rows = pl.ds(half * 128, 128)
@@ -322,9 +353,7 @@
                 value = value + rs_in[d, 3 - short, short].astype(F32)
         g = gcol[rows, :]
         for t in range(8):
-            dwv[rows, pl.ds(t * 128, 128)] = (value[:, t * 128 : t * 128 + 128] * g).astype(BF16)
-    store_dw = pltpu.make_async_copy(dwv, dw_out, st.at[4])
-    store_dw.start()
+            dw_out[rows, pl.ds(t * 128, 128)] = (value[:, t * 128 : t * 128 + 128] * g).astype(BF16)
 
     for chain in chains:
         for n in range(1, 5 - chain[2]):
@@ -346,29 +375,33 @@
         d1_copy(q).wait_send()
         d3_copy(q).wait_send()
     d2_copy.wait_send()
-    store_mw.wait()
-    store_mm.wait()
-    store_dx.wait()
-    store_kv.wait()
-    store_dw.wait()
+
+
+def finish(*refs):
+    copies = [pltpu.make_async_copy(refs[i], refs[6 + i], refs[12].at[i]) for i in range(6)]
+    for copy in copies:
+        copy.start()
+    for copy in copies:
+        copy.wait()
 
 
 def local(hidden, norm_gain, weight, upstream, global_weight, global_momentum, replica_delta):
     anywhere = pl.BlockSpec(memory_space=pl.ANY)
     in_vmem = pl.BlockSpec(memory_space=pltpu.VMEM)
+    in_hbm = pl.BlockSpec(memory_space=pltpu.HBM)
     dma = pltpu.SemaphoreType.DMA
-    kv, dx, dw, gg, mw, mm = pl.pallas_call(
+    results = pl.pallas_call(
         kernel,
         out_shape=(
-            jax.ShapeDtypeStruct((T, K), BF16),
-            jax.ShapeDtypeStruct((T, D), BF16),
-            jax.ShapeDtypeStruct((F, K), BF16),
-            jax.ShapeDtypeStruct((1, F), F32),
-            jax.ShapeDtypeStruct((F, K), F32),
-            jax.ShapeDtypeStruct((F, K), F32),
+            pltpu.VMEM((T, K), BF16),
+            pltpu.VMEM((T, D), BF16),
+            pltpu.VMEM((F, K), BF16),
+            pltpu.VMEM((1, F), BF16),
+            pltpu.VMEM((F, K), F32),
+            pltpu.VMEM((F, K), F32),
         ),
-        in_specs=[anywhere, in_vmem] + [anywhere] * 5,
-        out_specs=(anywhere, anywhere, anywhere, in_vmem, anywhere, anywhere),
+        in_specs=[in_hbm, in_vmem] + [in_hbm] * 5,
+        out_specs=(in_vmem,) * 6,
         scratch_shapes=[
             pltpu.VMEM((T, D), BF16),
             pltpu.VMEM((8, 4 * T, F), BF16),
@@ -394,24 +427,31 @@
             pltpu.VMEM((F, K), BF16),
             pltpu.VMEM((F, K), F32),
             pltpu.VMEM((F, K), F32),
-            pltpu.VMEM((T, D), BF16),
-            pltpu.VMEM((F, K), BF16),
             pltpu.VMEM((T, K), F32),
-            dma((6,)), dma((8,)), dma((5,)),
+            dma((6,)), dma((8,)),
             dma((2, 4, 2)), dma((2, 4, 2)), dma((2, 4, 2)), dma((2, 4, 2)),
             dma((3, 8)), dma((3, 8)), dma((3,)), dma((3,)), dma((3, 8)), dma((3, 8)),
             dma((3,)), dma((3,)), dma((7,)), dma((7,)),
             dma((3,)), dma((3,)), dma, dma, dma((3,)), dma((3,)),
         ],
         compiler_params=pltpu.CompilerParams(
-            collective_id=0, has_side_effects=True, vmem_limit_bytes=58 * 2**20
+            collective_id=0, has_side_effects=True, vmem_limit_bytes=59 * 2**20
         ),
         cost_estimate=pl.CostEstimate(flops=6442450944, bytes_accessed=14 * 2**20, transcendentals=0),
         name="project",
     )(
         hidden[0], norm_gain, weight[0], upstream[0], replica_delta[0], global_weight, global_momentum
     )
-    return kv[None], dx[None], dw[None], gg.astype(BF16), mw, mm
+    kv, dx, dw, gg, mw, mm = pl.pallas_call(
+        finish,
+        out_shape=tuple(jax.ShapeDtypeStruct(r.shape, r.dtype) for r in results),
+        in_specs=[in_vmem] * 6,
+        out_specs=(anywhere,) * 6,
+        scratch_shapes=[dma((6,))],
+        compiler_params=pltpu.CompilerParams(vmem_limit_bytes=8 * 2**20),
+        name="finish",
+    )(*results)
+    return kv[None], dx[None], dw[None], gg, mw, mm
 
 
 def solution(mesh):

time: 111 us -> 97.4 us (0.88)
  local copies, waits for them, and re-layouts: 7.63 us -> 0 us
  Pallas kernels: 102 us -> 96.7 us
  other arithmetic: 1.24 us -> 0 us
    unnamed x11 -> x0, local copies, waits for them, and re-layouts: 7.63 us -> none
    pallas_call x1 -> x2, Pallas kernels: 102 us -> 96.7 us  [the longest x1 94.3 us: local(): pl.pallas_call(kernel, out_shape=(pltpu.VMEM((T, K), BF16), pltpu.VMEM((T...]
    convert_element_type x1 -> x0, other arithmetic: 1.24 us -> none  [local(): return (kv[None], dx[None], dw[None], gg.astype(BF16), mw, mm)]
where the time goes in v2:
time: 97.4 us; the launch traced here: 97.3 us
  Pallas kernels  96.7 us (99%)
    pallas_call x1, Pallas kernels, local(): pl.pallas_call(kernel, out_shape=(pltpu.VMEM((T, K), BF16), pltpu.VMEM((T...  94.3 us
    pallas_call x1, Pallas kernels, local(): pl.pallas_call(finish, out_shape=tuple((jax.ShapeDtypeStruct(r.shape, r.d...  2.32 us

profile of v2, /device:TPU:8, one launch (start us, length us, event | category | flops | bytes accessed | tf_op | source)
XLA Modules:
  0.0 97.3 jit_solution(7464794885248744814)
XLA Ops:
  0.6 94.3 %project.1 = (bf16[128,1024]{1,0:T(8,128)(2,1)S(1)}, bf16[128,8192]{1,0:T(8,128)(2,1)S(1)}, bf16[256,1024]{1,0:T(8,128)(2,1)S(1)}, bf16[1,256]{1,0:T(2,128)(2,1)...) custom-call(bf16[128,8192]{1,0:T(8,128)(2,1)} %bitcast.7, bf16[1,256]{1,0:T(2,128)(2,1)} %gain_ref.1, ...), custom_call_target="tpu_custom_call" | custom-call | flops 6442450944 | bytes 14680064 | tf_op jit(solution)/shard_map/project/pallas_call | solution.py:393
  95.0 2.3 %finish.1 = (bf16[128,1024]{1,0:T(8,128)(2,1)}, bf16[128,8192]{1,0:T(8,128)(2,1)}, bf16[256,1024]{1,0:T(8,128)(2,1)}, bf16[1,256]{1,0:T(2,128)(2,1)}, f32[256,1024]{1,0:T(8,128)}, /*index=5*/f32[256,1024]{1,0:T(8,128)}) custom-call(bf16[128,1024]{1,0:T(8,128)(2,1)S(1)} %get-tuple-element.18.refs_0_, bf16[128,8192]{1,0:T(8,128)(2,1)S(1)} %get-tuple-element.19.refs_1_, ...), custom_call_target="tpu_custom_call" | custom-call | tf_op jit(solution)/shard_map/finish/pallas_call | solution.py:445

commit v3 on v2

--- a/solution.py
+++ b/solution.py
@@ -24,9 +24,9 @@
 def kernel(
     x_hbm, gain_ref, w_hbm, u_hbm, delta_hbm, gw_hbm, gm_hbm,
     kv_out, dx_out, dw_out, gg_out, mw_out, mm_out,
-    xv, xq, wv, wq, uv, uall, ub, uh, inv, gcol, rs_out, rs_in,
-    kvs, kvr, gps, gpr, dv, dbf, d1, d2s, d2r, davg, gwv, gmv, kvv,
-    ld, lq, ag_s, ag_r, rs_s, rs_r, x_s, x_r, u_s, u_r, b_s, b_r, k_s, k_r, g_s, g_r,
+    xv, xq, wq, uv, uall, ub, uh, inv, gcol, rs_out, rs_in,
+    kvs, kvr, gps, gpr, gall, sums, dv, dbf, d1, d2s, d2r, davg, gwv, gmv, kvv,
+    ld, lq, ag_s, ag_r, rs_s, rs_r, x_s, x_r, u_s, u_r, b_s, b_r, k_s, k_r, g_s, g_r, n_s, n_r,
     d1_s, d1_r, d2_s, d2_r, d3_s, d3_r,
 ):
     fsdp, rep = lax.axis_index("fsdp"), lax.axis_index("replica")
@@ -48,16 +48,15 @@
             src_ref=src, dst_ref=dst, send_sem=s, recv_sem=r, device_id=to, device_id_type=MESH
         )
 
-    load_w = pltpu.make_async_copy(w_hbm, wv, ld.at[0])
+    def w_half(half):
+        return w_hbm.at[pl.ds(half * 128, 128)]
+
+    load_w = [pltpu.make_async_copy(w_half(i), wq.at[z, i], ld.at[6 * i]) for i in range(2)]
     load_u = pltpu.make_async_copy(u_hbm, uv, ld.at[1])
     load_x = pltpu.make_async_copy(x_hbm, xv, ld.at[2])
     load_d = pltpu.make_async_copy(delta_hbm, dv, ld.at[3])
     load_gw = pltpu.make_async_copy(gw_hbm, gwv, ld.at[4])
     load_gm = pltpu.make_async_copy(gm_hbm, gmv, ld.at[5])
-    load_w.start()
-    load_x.start()
-    load_u.start()
-    load_d.start()
 
     def own_x(j):
         return pltpu.make_async_copy(x_hbm.at[:, column(0, j)], xq.at[j, pl.ds(0, T)], lq.at[j])
@@ -69,15 +68,13 @@
     for to in others:
         pl.semaphore_signal(barrier, inc=1, device_id=to, device_id_type=MESH)
 
+    load_x.start()
+    load_u.start()
+    load_d.start()
+    for copy in load_w:
+        copy.start()
     gain_row = gain_ref[...].astype(F32)
-    gcol[...] = jnp.transpose(jnp.broadcast_to(gain_row, (128, F)))
-    load_w.wait()
-    for half in range(2):
-        rows = pl.ds(half * 128, 128)
-        g = gcol[rows, :]
-        for t in range(8):
-            cols = pl.ds(t * 128, 128)
-            wq[z, half, :, cols] = (wv[rows, cols].astype(F32) * g).astype(BF16)
+    gall[z] = gain_row
     pl.semaphore_wait(barrier, len(others))
 
     chains = [(1, 0, 0), (-1, 1, 0), (1, 1, 1), (-1, 0, 1)]
@@ -86,7 +83,7 @@
         sign, half, short = chain
         d = 0 if sign > 0 else 1
         block = wq.at[(z + 8 - sign * (n - 1)) % 8, half]
-        return remote(block, block, ag_s.at[d, n - 1, half], ag_r.at[d, n - 1, half], along(sign))
+        return remote(w_half(half) if n == 1 else block, block, ag_s.at[d, n - 1, half], ag_r.at[d, n - 1, half], along(sign))
 
     def gather_in(n, chain):
         sign, half, short = chain
@@ -96,6 +93,17 @@
 
     for chain in chains:
         gather(1, chain).start()
+
+    def n_copy(s, owner):
+        block = gall.at[(z + 8 + owner) % 8]
+        return remote(block, block, n_s.at[s - 1], n_r.at[s - 1], along(s))
+
+    for s in range(1, 8):
+        n_copy(s, 0).start()
+
+    def gain_of(*steps):
+        for step in steps:
+            n_copy((-step) % 8, step).wait_recv()
 
     def x_copy(k, j):
         return remote(
@@ -161,6 +169,7 @@
             j = (z + 8 + step) % 8
             w = wq[j].reshape(F, K)
             u = lax.dot_general(uall[...], w, (((1,), (1,)), ((), ())), preferred_element_type=F32)
+            u = u * gall[j]
             ub[j] = u.astype(BF16).reshape(4, T, F)
             for k in (2, 3, 1):
                 b_copy(k, j).start()
@@ -171,6 +180,7 @@
             j = (z + 8 + step - 2 * step * i) % 8
             w = wq[j].reshape(F, K)
             u = lax.dot_general(uall[...], w, (((1,), (1,)), ((), ())), preferred_element_type=F32)
+            u = u * gall[j]
             ub[j] = u.astype(BF16).reshape(4, T, F)
             for k in (2, 3, 1):
                 b_copy(k, j).start()
@@ -195,6 +205,9 @@
     u_copy(3).start()
     u_copy(1).wait_recv()
     u_copy(3).wait_recv()
+    for copy in load_w:
+        copy.wait()
+    gain_of(-1, 1)
     upper(-1, 2)
 
     hop(2)
@@ -207,9 +220,11 @@
     davg[quarter(xx), :] = ((d2s[...].astype(F32) + d2r[...].astype(F32)) * 0.125).astype(BF16)
     for q in range(1, 4):
         d3_copy(q).start()
+    gain_of(-2, 2)
     upper_pair(2)
 
     hop(3)
+    gain_of(-3, 3)
     upper_pair(3)
 
     def d3_in(q):
@@ -242,11 +257,15 @@
             rs_s.at[d, n - 1, short], rs_r.at[d, n - 1, short], along(sign),
         )
 
+    def prepare(n):
+        for i, (sign, half, short) in enumerate(chains):
+            if n < 5 - short:
+                sums[i] = partial((z + 8 + sign * (5 - short - n)) % 8, half)
+
     def send_sum(n, chain):
         sign, half, short = chain
         d = 0 if sign > 0 else 1
-        j = (z + 8 + sign * (5 - short - n)) % 8
-        value = partial(j, half)
+        value = sums[chains.index(chain)]
         if n > 1:
             reduce(n - 1, chain).wait_recv()
             value = value + rs_in[d, n - 2, short].astype(F32)
@@ -259,12 +278,14 @@
         for k in (1, 2, 3):
             x_copy(k, j).wait_recv()
 
+    prepare(1)
     for chain in chains:
         send_sum(1, chain)
 
     for chain in chains[:2]:
         gather_in(4, chain).wait_recv()
 
+    gain_of(4)
     upper(4, 5)
 
     @pl.loop(0, 8)
@@ -278,6 +299,7 @@
     for s in range(1, 8):
         g_copy(s).start()
 
+    prepare(2)
     for chain in chains:
         send_sum(2, chain)
 
@@ -287,9 +309,8 @@
 
     def kv_part(k):
         def add(j, acc):
-            return acc + jnp.dot(
-                xq[j, pl.ds(k * T, T), :], wq[j].reshape(F, K), preferred_element_type=F32
-            )
+            x = (xq[j, pl.ds(k * T, T), :].astype(F32) * gall[j]).astype(BF16)
+            return acc + jnp.dot(x, wq[j].reshape(F, K), preferred_element_type=F32)
 
         return lax.fori_loop(0, 8, add, jnp.zeros((T, K), F32))
 
@@ -303,6 +324,7 @@
     k_copy(2).start()
     kvv[...] = kv_part(0)
 
+    prepare(3)
     for chain in chains:
         send_sum(3, chain)
 
@@ -327,8 +349,13 @@
             u = (ub[j, 0] if k == 0 else uh[k, j]).astype(F32)
             dx_out[:, column(k, j)] = (u - xv[:, column(k, j)].astype(F32) * coefficient).astype(BF16)
 
+    prepare(4)
     for chain in chains[:2]:
         send_sum(4, chain)
+
+    for half in range(2):
+        sums[half] = partial(z, half)
+    gcol[...] = jnp.transpose(jnp.broadcast_to(gain_row, (128, F)))
 
     for k in (1, 2):
         k_copy(k).wait_recv()
@@ -344,7 +371,7 @@
 
     for half in range(2):
         rows = pl.ds(half * 128, 128)
-        value = partial(z, half)
+        value = sums[half]
         for chain in chains:
             if chain[1] == half:
                 sign, _, short = chain
@@ -371,6 +398,7 @@
 
     for s in range(1, 8):
         g_copy(s).wait_send()
+        n_copy(s, 0).wait_send()
     for q in range(1, 4):
         d1_copy(q).wait_send()
         d3_copy(q).wait_send()
@@ -378,7 +406,12 @@
 
 
 def finish(*refs):
-    copies = [pltpu.make_async_copy(refs[i], refs[6 + i], refs[12].at[i]) for i in range(6)]
+    copies = []
+    for i, parts in enumerate((1, 4, 1, 1, 2, 2)):
+        rows = refs[i].shape[0] // parts
+        for part in range(parts):
+            at = pl.ds(part * rows, rows)
+            copies.append(pltpu.make_async_copy(refs[i].at[at], refs[6 + i].at[at], refs[12].at[len(copies)]))
     for copy in copies:
         copy.start()
     for copy in copies:
@@ -405,7 +438,6 @@
         scratch_shapes=[
             pltpu.VMEM((T, D), BF16),
             pltpu.VMEM((8, 4 * T, F), BF16),
-            pltpu.VMEM((F, K), BF16),
             pltpu.VMEM((8, 2, 128, K), BF16),
             pltpu.VMEM((T, K), BF16),
             pltpu.VMEM((4 * T, K), BF16),
@@ -419,6 +451,8 @@
             pltpu.VMEM((3, T, K), BF16),
             pltpu.VMEM((8, 1, F), F32),
             pltpu.VMEM((7, 1, F), F32),
+            pltpu.VMEM((8, 1, F), F32),
+            pltpu.VMEM((4, 128, K), F32),
             pltpu.VMEM((F, K), F32),
             pltpu.VMEM((F, K), BF16),
             pltpu.VMEM((3, R, K), BF16),
@@ -428,10 +462,10 @@
             pltpu.VMEM((F, K), F32),
             pltpu.VMEM((F, K), F32),
             pltpu.VMEM((T, K), F32),
-            dma((6,)), dma((8,)),
+            dma((7,)), dma((8,)),
             dma((2, 4, 2)), dma((2, 4, 2)), dma((2, 4, 2)), dma((2, 4, 2)),
             dma((3, 8)), dma((3, 8)), dma((3,)), dma((3,)), dma((3, 8)), dma((3, 8)),
-            dma((3,)), dma((3,)), dma((7,)), dma((7,)),
+            dma((3,)), dma((3,)), dma((7,)), dma((7,)), dma((7,)), dma((7,)),
             dma((3,)), dma((3,)), dma, dma, dma((3,)), dma((3,)),
         ],
         compiler_params=pltpu.CompilerParams(
@@ -447,7 +481,7 @@
         out_shape=tuple(jax.ShapeDtypeStruct(r.shape, r.dtype) for r in results),
         in_specs=[in_vmem] * 6,
         out_specs=(anywhere,) * 6,
-        scratch_shapes=[dma((6,))],
+        scratch_shapes=[dma((11,))],
         compiler_params=pltpu.CompilerParams(vmem_limit_bytes=8 * 2**20),
         name="finish",
     )(*results)

time: 97.4 us -> 97.1 us (level)
  no operation moved by 1% of the time
where the time goes in v3:
time: 97.1 us; the launch traced here: 97 us
  Pallas kernels  96.4 us (99%)
    pallas_call x1, Pallas kernels, local(): pl.pallas_call(kernel, out_shape=(pltpu.VMEM((T, K), BF16), pltpu.VMEM((T...  94 us
    pallas_call x1, Pallas kernels, local(): pl.pallas_call(finish, out_shape=tuple((jax.ShapeDtypeStruct(r.shape, r.d...  2.36 us

profile of v3, /device:TPU:8, one launch (start us, length us, event | category | flops | bytes accessed | tf_op | source)
XLA Modules:
  0.0 97.0 jit_solution(16042921704842485629)
XLA Ops:
  0.6 94.0 %project.1 = (bf16[128,1024]{1,0:T(8,128)(2,1)S(1)}, bf16[128,8192]{1,0:T(8,128)(2,1)S(1)}, bf16[256,1024]{1,0:T(8,128)(2,1)S(1)}, bf16[1,256]{1,0:T(2,128)(2,1)...) custom-call(bf16[128,8192]{1,0:T(8,128)(2,1)} %bitcast.7, bf16[1,256]{1,0:T(2,128)(2,1)} %gain_ref.1, ...), custom_call_target="tpu_custom_call" | custom-call | flops 6442450944 | bytes 14680064 | tf_op jit(solution)/shard_map/project/pallas_call | solution.py:426
  94.7 2.4 %finish.1 = (bf16[128,1024]{1,0:T(8,128)(2,1)}, bf16[128,8192]{1,0:T(8,128)(2,1)}, bf16[256,1024]{1,0:T(8,128)(2,1)}, bf16[1,256]{1,0:T(2,128)(2,1)}, f32[256,1024]{1,0:T(8,128)}, /*index=5*/f32[256,1024]{1,0:T(8,128)}) custom-call(bf16[128,1024]{1,0:T(8,128)(2,1)S(1)} %get-tuple-element.18.refs_0_, bf16[128,8192]{1,0:T(8,128)(2,1)S(1)} %get-tuple-element.19.refs_1_, ...), custom_call_target="tpu_custom_call" | custom-call | tf_op jit(solution)/shard_map/finish/pallas_call | solution.py:479

commit v4 on v3

--- a/solution.py
+++ b/solution.py
@@ -27,7 +27,7 @@
     xv, xq, wq, uv, uall, ub, uh, inv, gcol, rs_out, rs_in,
     kvs, kvr, gps, gpr, gall, sums, dv, dbf, d1, d2s, d2r, davg, gwv, gmv, kvv,
     ld, lq, ag_s, ag_r, rs_s, rs_r, x_s, x_r, u_s, u_r, b_s, b_r, k_s, k_r, g_s, g_r, n_s, n_r,
-    d1_s, d1_r, d2_s, d2_r, d3_s, d3_r,
+    d1_s, d1_r, d2_s, d2_r, d3_s, d3_r, ready,
 ):
     fsdp, rep = lax.axis_index("fsdp"), lax.axis_index("replica")
     h, z, c = fsdp // 16, (fsdp % 16) // 2, fsdp % 2
@@ -62,11 +62,14 @@
         return pltpu.make_async_copy(x_hbm.at[:, column(0, j)], xq.at[j, pl.ds(0, T)], lq.at[j])
 
     barrier = pltpu.get_barrier_semaphore()
-    others = [along(s) for s in range(1, 8)] + [mate(k) for k in range(1, 4)]
-    others += [device(h, z, c, low, (xx + q) % 4) for q in range(1, 4)]
-    others += [device(h, z, c, 1 - low, xx)]
-    for to in others:
+    hubs = [device(1 - h, z, 1, low, xx), device(h, z, 1, 1 - low, xx)]
+    hubs += [device(h, z, 1, low, (xx + q) % 4) for q in range(1, 4)]
+    for to in [along(1), along(-1)] + hubs:
         pl.semaphore_signal(barrier, inc=1, device_id=to, device_id_type=MESH)
+
+    @pl.when(c == 0)
+    def _():
+        pl.semaphore_signal(barrier, inc=1, device_id=mate(1), device_id_type=MESH)
 
     load_x.start()
     load_u.start()
@@ -75,7 +78,14 @@
         copy.start()
     gain_row = gain_ref[...].astype(F32)
     gall[z] = gain_row
-    pl.semaphore_wait(barrier, len(others))
+    @pl.when(c == 0)
+    def _():
+        pl.semaphore_wait(barrier, 2)
+
+    @pl.when(c == 1)
+    def _():
+        pl.semaphore_wait(barrier, 3 + 2 * len(hubs))
+        pl.semaphore_signal(ready, inc=1, device_id=mate(1), device_id_type=MESH)
 
     chains = [(1, 0, 0), (-1, 1, 0), (1, 1, 1), (-1, 0, 1)]
 
@@ -94,16 +104,17 @@
     for chain in chains:
         gather(1, chain).start()
 
-    def n_copy(s, owner):
-        block = gall.at[(z + 8 + owner) % 8]
-        return remote(block, block, n_s.at[s - 1], n_r.at[s - 1], along(s))
-
-    for s in range(1, 8):
-        n_copy(s, 0).start()
-
-    def gain_of(*steps):
-        for step in steps:
-            n_copy((-step) % 8, step).wait_recv()
+    def n_copy(n, sign, arriving=0):
+        d = 0 if sign > 0 else 1
+        block = gall.at[(z + 8 - sign * (n - 1 + arriving)) % 8]
+        return remote(block, block, n_s.at[d, n - 1], n_r.at[d, n - 1], along(sign))
+
+    for sign in (1, -1):
+        n_copy(1, sign).start()
+
+    @pl.when(c == 0)
+    def _():
+        pl.semaphore_wait(ready, 1)
 
     def x_copy(k, j):
         return remote(
@@ -190,6 +201,10 @@
             gather_in(n, chain).wait_recv()
             if n < 3 or chain[2] == 0:
                 gather(n + 1, chain).start()
+        for sign in (1, -1):
+            n_copy(n, sign, 1).wait_recv()
+            if n < 3 or sign > 0:
+                n_copy(n + 1, sign).start()
 
     hop(1)
 
@@ -207,7 +222,6 @@
     u_copy(3).wait_recv()
     for copy in load_w:
         copy.wait()
-    gain_of(-1, 1)
     upper(-1, 2)
 
     hop(2)
@@ -220,29 +234,7 @@
     davg[quarter(xx), :] = ((d2s[...].astype(F32) + d2r[...].astype(F32)) * 0.125).astype(BF16)
     for q in range(1, 4):
         d3_copy(q).start()
-    gain_of(-2, 2)
     upper_pair(2)
-
-    hop(3)
-    gain_of(-3, 3)
-    upper_pair(3)
-
-    def d3_in(q):
-        block = davg.at[quarter((xx + 4 - q) % 4)]
-        return remote(block, block, d3_s.at[q - 1], d3_r.at[q - 1], device(h, z, c, low, (xx + q) % 4))
-
-    for q in range(1, 4):
-        d3_in(q).wait_recv()
-    load_gw.wait()
-    load_gm.wait()
-
-    @pl.loop(0, 8)
-    def _(i):
-        rows = pl.ds(pl.multiple_of(i * 32, 32), 32)
-        average = davg[rows, :].astype(F32)
-        fresh = 0.9 * gmv[rows, :] + average
-        mm_out[rows, :] = fresh
-        mw_out[rows, :] = gwv[rows, :] - 0.7 * (average + 0.9 * fresh)
 
     def partial(j, half):
         return lax.dot_general(
@@ -272,20 +264,45 @@
         rs_out[d, n - 1, short] = value.astype(BF16)
         reduce(n, chain).start()
 
+    def first_sums():
+        @pl.loop(0, 8)
+        def _(j):
+            own_x(j).wait()
+            for k in (1, 2, 3):
+                x_copy(k, j).wait_recv()
+
+        prepare(1)
+        for chain in chains:
+            send_sum(1, chain)
+
+    pl.when(c == 0)(first_sums)
+
+    hop(3)
+    upper_pair(3)
+
+    def d3_in(q):
+        block = davg.at[quarter((xx + 4 - q) % 4)]
+        return remote(block, block, d3_s.at[q - 1], d3_r.at[q - 1], device(h, z, c, low, (xx + q) % 4))
+
+    for q in range(1, 4):
+        d3_in(q).wait_recv()
+    load_gw.wait()
+    load_gm.wait()
+
     @pl.loop(0, 8)
-    def _(j):
-        own_x(j).wait()
-        for k in (1, 2, 3):
-            x_copy(k, j).wait_recv()
-
-    prepare(1)
-    for chain in chains:
-        send_sum(1, chain)
+    def _(i):
+        rows = pl.ds(pl.multiple_of(i * 32, 32), 32)
+        average = davg[rows, :].astype(F32)
+        fresh = 0.9 * gmv[rows, :] + average
+        mm_out[rows, :] = fresh
+        mw_out[rows, :] = gwv[rows, :] - 0.7 * (average + 0.9 * fresh)
+
+    pl.when(c == 1)(first_sums)
 
     for chain in chains[:2]:
         gather_in(4, chain).wait_recv()
 
-    gain_of(4)
+    n_copy(4, 1, 1).wait_recv()
     upper(4, 5)
 
     @pl.loop(0, 8)
@@ -398,7 +415,7 @@
 
     for s in range(1, 8):
         g_copy(s).wait_send()
-        n_copy(s, 0).wait_send()
+        n_copy((s + 1) // 2, 1 if s % 2 else -1).wait_send()
     for q in range(1, 4):
         d1_copy(q).wait_send()
         d3_copy(q).wait_send()
@@ -465,8 +482,9 @@
             dma((7,)), dma((8,)),
             dma((2, 4, 2)), dma((2, 4, 2)), dma((2, 4, 2)), dma((2, 4, 2)),
             dma((3, 8)), dma((3, 8)), dma((3,)), dma((3,)), dma((3, 8)), dma((3, 8)),
-            dma((3,)), dma((3,)), dma((7,)), dma((7,)), dma((7,)), dma((7,)),
+            dma((3,)), dma((3,)), dma((7,)), dma((7,)), dma((2, 4)), dma((2, 4)),
             dma((3,)), dma((3,)), dma, dma, dma((3,)), dma((3,)),
+            pltpu.SemaphoreType.REGULAR,
         ],
         compiler_params=pltpu.CompilerParams(
             collective_id=0, has_side_effects=True, vmem_limit_bytes=59 * 2**20

time: 97.1 us -> 95.9 us (0.988)
  Pallas kernels: 96.4 us -> 94.6 us
    pallas_call x1, Pallas kernels: 94 us -> 92.3 us  [local(): pl.pallas_call(kernel, out_shape=(pltpu.VMEM((T, K), BF16), pltpu.VMEM((T...]
where the time goes in v4:
time: 95.9 us; the launch traced here: 95.3 us
  Pallas kernels  94.6 us (99%)
    pallas_call x1, Pallas kernels, local(): pl.pallas_call(kernel, out_shape=(pltpu.VMEM((T, K), BF16), pltpu.VMEM((T...  92.3 us
    pallas_call x1, Pallas kernels, local(): pl.pallas_call(finish, out_shape=tuple((jax.ShapeDtypeStruct(r.shape, r.d...  2.36 us

profile of v4, /device:TPU:8, one launch (start us, length us, event | category | flops | bytes accessed | tf_op | source)
XLA Modules:
  0.0 95.3 jit_solution(6605344318923233026)
XLA Ops:
  0.6 92.3 %project.1 = (bf16[128,1024]{1,0:T(8,128)(2,1)S(1)}, bf16[128,8192]{1,0:T(8,128)(2,1)S(1)}, bf16[256,1024]{1,0:T(8,128)(2,1)S(1)}, bf16[1,256]{1,0:T(2,128)(2,1)...) custom-call(bf16[128,8192]{1,0:T(8,128)(2,1)} %bitcast.7, bf16[1,256]{1,0:T(2,128)(2,1)} %gain_ref.1, ...), custom_call_target="tpu_custom_call" | custom-call | flops 6442450944 | bytes 14680064 | tf_op jit(solution)/shard_map/project/pallas_call | solution.py:443
  92.9 2.4 %finish.1 = (bf16[128,1024]{1,0:T(8,128)(2,1)}, bf16[128,8192]{1,0:T(8,128)(2,1)}, bf16[256,1024]{1,0:T(8,128)(2,1)}, bf16[1,256]{1,0:T(2,128)(2,1)}, f32[256,1024]{1,0:T(8,128)}, /*index=5*/f32[256,1024]{1,0:T(8,128)}) custom-call(bf16[128,1024]{1,0:T(8,128)(2,1)S(1)} %get-tuple-element.18.refs_0_, bf16[128,8192]{1,0:T(8,128)(2,1)S(1)} %get-tuple-element.19.refs_1_, ...), custom_call_target="tpu_custom_call" | custom-call | tf_op jit(solution)/shard_map/finish/pallas_call | solution.py:497

commit v5 on v4

--- a/solution.py
+++ b/solution.py
@@ -385,6 +385,29 @@
     for s in range(1, 8):
         gain_sum = gain_sum + gpr[s - 1]
     gg_out[...] = (gain_sum / gain_row).astype(BF16)
+
+    for chain in chains:
+        for n in range(1, 5 - chain[2]):
+            gather(n, chain).wait_send()
+            if n < 4 - chain[2]:
+                reduce(n, chain).wait_send()
+    for k in (1, 2, 3):
+        u_copy(k).wait_send()
+        k_copy(k).wait_send()
+
+    @pl.loop(0, 8)
+    def _(j):
+        for k in (1, 2, 3):
+            x_copy(k, j).wait_send()
+            b_copy(k, j).wait_send()
+
+    for s in range(1, 8):
+        g_copy(s).wait_send()
+        n_copy((s + 1) // 2, 1 if s % 2 else -1).wait_send()
+    for q in range(1, 4):
+        d1_copy(q).wait_send()
+        d3_copy(q).wait_send()
+    d2_copy.wait_send()
 
     for half in range(2):
         rows = pl.ds(half * 128, 128)
@@ -398,28 +421,8 @@
         g = gcol[rows, :]
         for t in range(8):
             dw_out[rows, pl.ds(t * 128, 128)] = (value[:, t * 128 : t * 128 + 128] * g).astype(BF16)
-
     for chain in chains:
-        for n in range(1, 5 - chain[2]):
-            gather(n, chain).wait_send()
-            reduce(n, chain).wait_send()
-    for k in (1, 2, 3):
-        u_copy(k).wait_send()
-        k_copy(k).wait_send()
-
-    @pl.loop(0, 8)
-    def _(j):
-        for k in (1, 2, 3):
-            x_copy(k, j).wait_send()
-            b_copy(k, j).wait_send()
-
-    for s in range(1, 8):
-        g_copy(s).wait_send()
-        n_copy((s + 1) // 2, 1 if s % 2 else -1).wait_send()
-    for q in range(1, 4):
-        d1_copy(q).wait_send()
-        d3_copy(q).wait_send()
-    d2_copy.wait_send()
+        reduce(4 - chain[2], chain).wait_send()
 
 
 def finish(*refs):

time: 95.9 us -> 95.7 us (level)
  no operation moved by 1% of the time
where the time goes in v5:
time: 95.7 us; the launch traced here: 95.1 us
  Pallas kernels  94.5 us (99%)
    pallas_call x1, Pallas kernels, local(): pl.pallas_call(kernel, out_shape=(pltpu.VMEM((T, K), BF16), pltpu.VMEM((T...  92.1 us
    pallas_call x1, Pallas kernels, local(): pl.pallas_call(finish, out_shape=tuple((jax.ShapeDtypeStruct(r.shape, r.d...  2.36 us

profile of v5, /device:TPU:8, one launch (start us, length us, event | category | flops | bytes accessed | tf_op | source)
XLA Modules:
  0.0 95.1 jit_solution(14696919790159280621)
XLA Ops:
  0.6 92.1 %project.1 = (bf16[128,1024]{1,0:T(8,128)(2,1)S(1)}, bf16[128,8192]{1,0:T(8,128)(2,1)S(1)}, bf16[256,1024]{1,0:T(8,128)(2,1)S(1)}, bf16[1,256]{1,0:T(2,128)(2,1)...) custom-call(bf16[128,8192]{1,0:T(8,128)(2,1)} %bitcast.7, bf16[1,256]{1,0:T(2,128)(2,1)} %gain_ref.1, ...), custom_call_target="tpu_custom_call" | custom-call | flops 6442450944 | bytes 14680064 | tf_op jit(solution)/shard_map/project/pallas_call | solution.py:446
  92.7 2.4 %finish.1 = (bf16[128,1024]{1,0:T(8,128)(2,1)}, bf16[128,8192]{1,0:T(8,128)(2,1)}, bf16[256,1024]{1,0:T(8,128)(2,1)}, bf16[1,256]{1,0:T(2,128)(2,1)}, f32[256,1024]{1,0:T(8,128)}, /*index=5*/f32[256,1024]{1,0:T(8,128)}) custom-call(bf16[128,1024]{1,0:T(8,128)(2,1)S(1)} %get-tuple-element.18.refs_0_, bf16[128,8192]{1,0:T(8,128)(2,1)S(1)} %get-tuple-element.19.refs_1_, ...), custom_call_target="tpu_custom_call" | custom-call | tf_op jit(solution)/shard_map/finish/pallas_call | solution.py:500
